TPU v7x, 32 devices: a whole 2x2x4 slice. The times are simulated.
32 devices in a mesh: groups: 2 (over x), wide: 16 (over z, y, core).
Axes of the slice: x: 2, y: 2, z: 4, core: 2. Of those that a mesh axis runs over, the one named last changes fastest.
Arguments:
- residual: bfloat16 [128, 8192], P(('groups', 'wide')), parts along dimension 0
- norm_gain: float32 [8192], replicated, may hold values from 0.1 to 1.9
- query_weight: bfloat16 [8192, 8192], P(None, 'wide'), may hold values from -0.0625 to 0.0625
- key_weight: bfloat16 [8192, 1024], P(None, 'wide'), may hold values from -0.0625 to 0.0625
- value_weight: bfloat16 [8192, 1024], P(None, 'wide'), may hold values from -0.0625 to 0.0625
- output_weight: bfloat16 [8192, 8192], P(None, 'wide'), may hold values from -0.0625 to 0.0625
- past_cache: bfloat16 [128, 2, 8, 512, 128], P(('groups', 'wide')), parts along dimension 0, as said below
- lengths: int32 [128], P(('groups', 'wide')), parts along dimension 0, may hold values from 1 to 512, 16384 in all
Outputs:
- final_state: bfloat16 [128, 8192], P(('groups', 'wide')), parts along dimension 0
- new_entries: bfloat16 [128, 2, 2048], P(('groups', 'wide')), parts along dimension 0
There are 2 independent parts, one for each index of `groups`. A program takes and returns all parts, laid end to end along the dimension named above; an argument that names none is the same for every part. Nothing has to cross between parts.
Inputs may be any that keep to these rules, and one draw needn't show every extreme that they name: past_cache[r, 0] holds robot r's cached keys, already rotated to their positions; past_cache[r, 1] its values. lengths[r] slots of robot r's 512 are filled, from slot 0 on; some robot fills all.
All inputs are finite; a program needn't handle non-finite values. No bound on the sum of `lengths` on one device may be relied on, other than what follows from the above.
Results may differ from a plain program's by a relative error of at most 0.02.
The roundings to bfloat16 on the way count: a program that leaves them out, or rounds other values in their place, can miss the bound.
Values may be sent and summed in bfloat16 or wider, within the bound.
A program may use at most 128 MiB of HBM per device.

v0:
```python
import math

import jax
import jax.numpy as jnp
from jax import lax
from jax.sharding import PartitionSpec as P

QH = 64
KVH = 8
HD = 128
STEPS = 2


rope_base = 500000.0
norm_eps = 1e-05


def rotate_heads(heads_block, positions):
    head_size = heads_block.shape[-1]
    half_size = head_size // 2
    frequency = rope_base ** (-2.0 * jnp.arange(half_size, dtype=jnp.float32) / head_size)
    angles = positions.astype(jnp.float32)[:, None, None] * frequency[None, None, :]
    cosine = jnp.cos(angles)
    sine_part = jnp.sin(angles)
    values = heads_block.astype(jnp.float32)
    first_half = values[..., :half_size]
    second = values[..., half_size:]
    return jnp.concatenate(
        [first_half * cosine - second * sine_part, second * cosine + first_half * sine_part],
        axis=-1,
    ).astype(jnp.bfloat16)


def attend_local(queries, past_cache, fresh_keys, fresh_values, lengths, step_now):
    robots_here, head_count, head_size = queries.shape
    kv_heads = past_cache.shape[2]
    grouped = queries.reshape(robots_here, kv_heads, head_count // kv_heads, head_size)
    score_scale = 1.0 / math.sqrt(head_size)
    past_scores = (
        jnp.einsum("rkgd,rkcd->rkgc", grouped, past_cache[:, 0], preferred_element_type=jnp.float32)
        * score_scale
    )
    fresh_scores = (
        jnp.einsum("rkgd,rskd->rkgs", grouped, fresh_keys, preferred_element_type=jnp.float32)
        * score_scale
    )
    slot_index = jnp.arange(past_cache.shape[3], dtype=jnp.int32)
    past_scores = jnp.where(
        slot_index[None, None, None, :] < lengths[:, None, None, None], past_scores, -jnp.inf
    )
    turn_index = jnp.arange(fresh_keys.shape[1], dtype=jnp.int32)
    fresh_scores = jnp.where(turn_index[None, None, None, :] <= step_now, fresh_scores, -jnp.inf)
    peak_score = jnp.maximum(jnp.max(past_scores, axis=-1), jnp.max(fresh_scores, axis=-1))
    past_exp = jnp.exp(past_scores - peak_score[..., None])
    fresh_exp = jnp.exp(fresh_scores - peak_score[..., None])
    denominator = jnp.sum(past_exp, axis=-1) + jnp.sum(fresh_exp, axis=-1)
    past_weights = (past_exp / denominator[..., None]).astype(jnp.bfloat16)
    fresh_weights = (fresh_exp / denominator[..., None]).astype(jnp.bfloat16)
    context = jnp.einsum(
        "rkgc,rkcd->rkgd", past_weights, past_cache[:, 1], preferred_element_type=jnp.float32
    )
    context = context + jnp.einsum(
        "rkgs,rskd->rkgd", fresh_weights, fresh_values, preferred_element_type=jnp.float32
    )
    return context.reshape(robots_here, head_count * head_size).astype(jnp.bfloat16)


def local(
    residual, norm_gain, query_weight, key_weight, value_weight, output_weight, past_cache, lengths
):
    group_size = lax.axis_size("wide")
    robots_here, width = residual.shape
    query_cols = query_weight.shape[1]
    kv_cols = key_weight.shape[1]
    fresh_keys = jnp.zeros((robots_here, STEPS, KVH, HD), jnp.bfloat16)
    fresh_values = jnp.zeros((robots_here, STEPS, KVH, HD), jnp.bfloat16)
    final_state = residual
    for step_now in range(STEPS):
        widened = final_state.astype(jnp.float32)
        inverse_rms = lax.rsqrt(jnp.sum(widened * widened, axis=1) / width + norm_eps)
        normed = (widened * inverse_rms[:, None] * norm_gain[None, :]).astype(jnp.bfloat16)
        project_segment = lax.all_gather(normed, "wide", axis=0, tiled=True)
        projected = jnp.concatenate(
            [
                jnp.dot(project_segment, query_weight, preferred_element_type=jnp.float32),
                jnp.dot(project_segment, key_weight, preferred_element_type=jnp.float32),
                jnp.dot(project_segment, value_weight, preferred_element_type=jnp.float32),
            ],
            axis=1,
        ).astype(jnp.bfloat16)
        attend_fresh_keys = fresh_keys
        attend_fresh_values = fresh_values
        arrived = lax.all_to_all(projected, "wide", split_axis=0, concat_axis=1, tiled=True)
        blocks = arrived.reshape(robots_here, group_size, query_cols + 2 * kv_cols)
        positions = lengths + step_now
        queries = rotate_heads(blocks[:, :, :query_cols].reshape(robots_here, QH, HD), positions)
        new_keys = rotate_heads(
            blocks[:, :, query_cols : query_cols + kv_cols].reshape(robots_here, KVH, HD), positions
        )
        new_values = blocks[:, :, query_cols + kv_cols :].reshape(robots_here, KVH, HD)
        attend_fresh_keys = attend_fresh_keys.at[:, step_now].set(new_keys)
        attend_fresh_values = attend_fresh_values.at[:, step_now].set(new_values)
        context = attend_local(
            queries, past_cache, attend_fresh_keys, attend_fresh_values, lengths, step_now
        )
        attended = jnp.dot(
            lax.all_gather(context, "wide", axis=0, tiled=True),
            output_weight,
            preferred_element_type=jnp.float32,
        ).astype(jnp.bfloat16)
        attended, fresh_keys, fresh_values = (attended, attend_fresh_keys, attend_fresh_values)
        returned = lax.all_to_all(attended, "wide", split_axis=0, concat_axis=1, tiled=True)
        final_state = (final_state.astype(jnp.float32) + returned.astype(jnp.float32)).astype(
            jnp.bfloat16
        )
    new_entries = jnp.concatenate(
        [
            fresh_keys.reshape(robots_here, STEPS, KVH * HD),
            fresh_values.reshape(robots_here, STEPS, KVH * HD),
        ],
        axis=2,
    )
    return (final_state, new_entries)


def solution(mesh):
    return jax.shard_map(
        local,
        mesh=mesh,
        in_specs=(
            P(("groups", "wide"), None),
            P(),
            P(None, "wide"),
            P(None, "wide"),
            P(None, "wide"),
            P(None, "wide"),
            P(("groups", "wide"), None, None, None, None),
            P(("groups", "wide")),
        ),
        out_specs=(P(("groups", "wide"), None), P(("groups", "wide"), None, None)),
        check_vma=False,
    )
```

profile of v0, /device:TPU:0, one launch (start us, length us, event | category | flops | bytes accessed | tf_op | source)
XLA Modules:
  0.0 255.9 jit_solution(12387314113408932245)
XLA Ops:
  8.3 1.6 fusion.57
  10.8 40.6 %all-gather.9.cloned.1.call-done = bf16[16,4,8192]{2,1,0:T(4,128)(2,1)} async-done(((bf16[1,4,8192]{2,1,0:T(4,128)(2,1)}), bf16[16,4,8192]{2,1,0:T(4,128)(2,1)}) %all-gather.9.cloned.1.call-update) | async-done | bytes 1048592 | tf_op jit(solution)/shard_map/all_gather | solution.py:82
  51.4 1.3 reshape.450
  53.2 1.6 convolution_convert_fusion.7
  54.9 4.9 %convolution_convert_fusion.3 = bf16[64,512]{1,0:T(8,128)(2,1)S(1)} fusion(bf16[64,8192]{1,0:T(8,128)(2,1)S(1)} %reshape.450, bf16[8192,512]{1,0:T(8,128)(2,1)} %param.18), kind=kOutput, calls=%fused_computation.23 | convolution fusion | flops 536903680 | bytes 9502720 | tf_op jit(solution)/shard_map/dot_general | solution.py:85
  60.5 3.6 %all-to-all-start = ((bf16[16,4,640]{2,1,0:T(4,128)(2,1)}), bf16[16,4,640]{2,1,0:T(4,128)(2,1)S(1)}, u32[]{:S(2)}, u32[]{:S(2)}) async-start(bf16[16,4,640]{2,1,0:T(4,128)(2,1)} %pad_maximum_fusion), calls=%async_computation | async-start | bytes 163840 | tf_op jit(solution)/shard_map/all_to_all | solution.py:93
  64.3 7.0 %all-to-all-done = bf16[16,4,640]{2,1,0:T(4,128)(2,1)S(1)} async-done(((bf16[16,4,640]{2,1,0:T(4,128)(2,1)}), bf16[16,4,640]{2,1,0:T(4,128)(2,1)S(1)}, u32[]{:S(2)}, u32[]{:S(2)}) %all-to-all-start) | async-done | bytes 81952 | tf_op jit(solution)/shard_map/all_to_all | solution.py:93
  72.2 3.5 %fusion.86 = (f32[4,8,8]{2,1,0:T(8,128)S(1)}, f32[4,8,8,512]{3,2,1,0:T(8,128)S(1)}) fusion(bf16[4,2,8,512,128]{4,3,2,1,0:T(8,128)(2,1)} %param.22, bf16[4,8,8,64]{3,2,1,0:T(8,128)(2,1)S(1)} %get-tuple-element.67, bf16[4,8,8,64]{3,2,1,0:T(8,128)(2,1)S(1)} %get-tuple-element.66, pred[4,512]{1,0:T(4,128)(4,1)S(1)} %iota_compare_fusion), kind=kOutput, calls=%fused_computation.125 | convolution fusion | flops 34078464 | bytes 4787200 | tf_op jit(solution)/shard_map/rkgd,rkcd->rkgc/dot_general | solution.py:40
  76.3 2.9 %fusion.33 = bf16[4,8,8,128]{3,2,1,0:T(8,128)(2,1)S(1)} fusion(f32[4,8,8,128]{3,2,1,0:T(8,128)S(1)} %fusion.60, bf16[4,2,8,512,128]{4,3,2,1,0:T(8,128)(2,1)} %param.22, f32[4,8,8,512]{3,2,1,0:T(8,128)S(1)} %get-tuple-element.85, f32[4,8,8]{2,1,0:T(8,128)S(1)} %add.70, f32[4,8,8]{2,1,0:T(8,128)S(1)} %max.14), kind=kOutput, calls=%fused_computation.19 | convolution fusion | flops 34013184 | bytes 4917248 | tf_op jit(solution)/shard_map/rkgc,rkcd->rkgd/dot_general | solution.py:59
  79.9 35.4 %all-gather.11.cloned.1.call-done = bf16[16,4,8192]{2,1,0:T(4,128)(2,1)} async-done(((bf16[1,4,8192]{2,1,0:T(4,128)(2,1)}), bf16[16,4,8192]{2,1,0:T(4,128)(2,1)}) %all-gather.11.cloned.1.call-update) | async-done | bytes 1048592 | tf_op jit(solution)/shard_map/all_gather | solution.py:107
  115.4 1.3 reshape.452
  116.7 5.0 %convolution_convert_fusion.2 = bf16[64,512]{1,0:T(8,128)(2,1)S(1)} fusion(bf16[64,8192]{1,0:T(8,128)(2,1)S(1)} %reshape.452, bf16[8192,512]{1,0:T(8,128)(2,1)} %param.21), kind=kOutput, calls=%fused_computation.22 | convolution fusion | flops 536903680 | bytes 9502720 | tf_op jit(solution)/shard_map/dot_general | solution.py:106
  121.8 10.3 %all_to_all.52 = bf16[16,4,512]{2,1,0:T(4,128)(2,1)S(1)} all-to-all(bf16[16,4,512]{2,1,0:T(4,128)(2,1)S(1)} %all_to_all.42), channel_id=1, replica_groups=mesh['groups'=2,'wide'=16] {'wide'}, dimensions={0} | all-to-all | bytes 131072 | tf_op jit(solution)/shard_map/all_to_all | solution.py:112
  133.1 35.4 %all-gather.13.cloned.1.call-done = bf16[16,4,8192]{2,1,0:T(4,128)(2,1)} async-done(((bf16[1,4,8192]{2,1,0:T(4,128)(2,1)}), bf16[16,4,8192]{2,1,0:T(4,128)(2,1)}) %all-gather.13.cloned.1.call-update) | async-done | bytes 1048592 | tf_op jit(solution)/shard_map/all_gather | solution.py:82
  168.5 1.3 reshape.454
  170.7 4.9 %convolution_convert_fusion.1 = bf16[64,512]{1,0:T(8,128)(2,1)S(1)} fusion(bf16[64,8192]{1,0:T(8,128)(2,1)S(1)} %reshape.454, bf16[8192,512]{1,0:T(8,128)(2,1)} %param.18), kind=kOutput, calls=%fused_computation.21 | convolution fusion | flops 536903680 | bytes 9502720 | tf_op jit(solution)/shard_map/dot_general | solution.py:85
  176.4 3.6 %all-to-all-start.2 = ((bf16[16,4,640]{2,1,0:T(4,128)(2,1)}), bf16[16,4,640]{2,1,0:T(4,128)(2,1)S(1)}, u32[]{:S(2)}, u32[]{:S(2)}) async-start(bf16[16,4,640]{2,1,0:T(4,128)(2,1)} %pad_maximum_fusion.1), calls=%async_computation.2 | async-start | bytes 163840 | tf_op jit(solution)/shard_map/all_to_all | solution.py:93
  180.1 7.1 %all-to-all-done.2 = bf16[16,4,640]{2,1,0:T(4,128)(2,1)S(1)} async-done(((bf16[16,4,640]{2,1,0:T(4,128)(2,1)}), bf16[16,4,640]{2,1,0:T(4,128)(2,1)S(1)}, u32[]{:S(2)}, u32[]{:S(2)}) %all-to-all-start.2) | async-done | bytes 81952 | tf_op jit(solution)/shard_map/all_to_all | solution.py:93
  187.8 3.5 %fusion.88 = (f32[4,8,8]{2,1,0:T(8,128)S(1)}, f32[4,8,8,512]{3,2,1,0:T(8,128)S(1)}) fusion(bf16[4,2,8,512,128]{4,3,2,1,0:T(8,128)(2,1)} %param.22, bf16[4,8,8,64]{3,2,1,0:T(8,128)(2,1)S(1)} %get-tuple-element.65, bf16[4,8,8,64]{3,2,1,0:T(8,128)(2,1)S(1)} %get-tuple-element.64, pred[4,512]{1,0:T(4,128)(4,1)S(1)} %iota_compare_fusion), kind=kOutput, calls=%fused_computation.127 | convolution fusion | flops 34078464 | bytes 4787200 | tf_op jit(solution)/shard_map/rkgd,rkcd->rkgc/dot_general | solution.py:40
  192.1 2.9 %fusion.30 = bf16[4,8,8,128]{3,2,1,0:T(8,128)(2,1)S(1)} fusion(f32[4,8,8,128]{3,2,1,0:T(8,128)S(1)} %fusion.61, bf16[4,2,8,512,128]{4,3,2,1,0:T(8,128)(2,1)} %param.22, f32[4,8,8,512]{3,2,1,0:T(8,128)S(1)} %get-tuple-element.89, f32[4,8,8]{2,1,0:T(8,128)S(1)} %add.77, f32[4,8,8]{2,1,0:T(8,128)S(1)} %max.15), kind=kOutput, calls=%fused_computation.18 | convolution fusion | flops 34013184 | bytes 4917248 | tf_op jit(solution)/shard_map/rkgc,rkcd->rkgd/dot_general | solution.py:59
  195.9 35.3 %all-gather.15.cloned.1.call-done = bf16[16,4,8192]{2,1,0:T(4,128)(2,1)} async-done(((bf16[1,4,8192]{2,1,0:T(4,128)(2,1)}), bf16[16,4,8192]{2,1,0:T(4,128)(2,1)}) %all-gather.15.cloned.1.call-update) | async-done | bytes 1048592 | tf_op jit(solution)/shard_map/all_gather | solution.py:107
  232.6 4.9 %convolution_convert_fusion = bf16[64,512]{1,0:T(8,128)(2,1)S(1)} fusion(bf16[64,8192]{1,0:T(8,128)(2,1)S(1)} %reshape.456, bf16[8192,512]{1,0:T(8,128)(2,1)} %param.21), kind=kOutput, calls=%fused_computation.20 | convolution fusion | flops 536903680 | bytes 9502720 | tf_op jit(solution)/shard_map/dot_general | solution.py:106
  238.2 3.6 %all-to-all-start.3 = ((bf16[16,4,512]{2,1,0:T(4,128)(2,1)}), bf16[16,4,512]{2,1,0:T(4,128)(2,1)S(1)}, u32[]{:S(2)}, u32[]{:S(2)}) async-start(bf16[16,4,512]{2,1,0:T(4,128)(2,1)} %all_to_all.46), calls=%async_computation.3 | async-start | bytes 131072 | tf_op jit(solution)/shard_map/all_to_all | solution.py:112
  242.5 6.2 %all-to-all-done.3 = bf16[16,4,512]{2,1,0:T(4,128)(2,1)S(1)} async-done(((bf16[16,4,512]{2,1,0:T(4,128)(2,1)}), bf16[16,4,512]{2,1,0:T(4,128)(2,1)S(1)}, u32[]{:S(2)}, u32[]{:S(2)}) %all-to-all-start.3) | async-done | bytes 65568 | tf_op jit(solution)/shard_map/all_to_all | solution.py:112
  (80 shorter events, 13.6 us)
Async XLA Ops:
  7.2 45.6 %copy-start = (bf16[8192,64]{0,1:T(8,128)(2,1)S(1)}, bf16[8192,64]{0,1:T(8,128)(2,1)}, u32[]{:S(2)}) copy-start(bf16[8192,64]{0,1:T(8,128)(2,1)} %param.20) | copy-start | bytes 3145732
  7.2 44.2 %all-gather.9.cloned.1.call-start = ((), (), s32[]{:S(2)}) async-start(), calls=%async_computation.4 | async-start | bytes 1114112 | tf_op jit(solution)/shard_map/all_gather | solution.py:82
  54.9 9.4 %copy-start.4 = (s32[4]{0:T(128)S(1)}, s32[4]{0:T(128)}, u32[]{:S(2)}) copy-start(s32[4]{0:T(128)} %param.23) | copy-start | bytes 52
  60.5 10.8 %all-to-all-start = ((bf16[16,4,640]{2,1,0:T(4,128)(2,1)}), bf16[16,4,640]{2,1,0:T(4,128)(2,1)S(1)}, u32[]{:S(2)}, u32[]{:S(2)}) async-start(bf16[16,4,640]{2,1,0:T(4,128)(2,1)} %pad_maximum_fusion), calls=%async_computation | async-start | bytes 163840 | tf_op jit(solution)/shard_map/all_to_all | solution.py:93
  64.2 51.2 %all-gather.11.cloned.1.call-start = ((), (), s32[]{:S(2)}) async-start(), calls=%async_computation.5 | async-start | bytes 1114112 | tf_op jit(solution)/shard_map/all_gather | solution.py:107
  79.9 88.6 %all-gather.13.cloned.1.call-start = ((), (), s32[]{:S(2)}) async-start(), calls=%async_computation.6 | async-start | bytes 1114112 | tf_op jit(solution)/shard_map/all_gather | solution.py:82
  116.7 15.4 %copy-start.2 = (bf16[4,8192]{1,0:T(4,128)(2,1)S(1)}, bf16[4,8192]{1,0:T(4,128)(2,1)}, u32[]{:S(2)}) copy-start(bf16[4,8192]{1,0:T(4,128)(2,1)} %param.16) | copy-start | bytes 196612
  116.7 15.6 %copy-start.3 = (f32[8192]{0:T(1024)S(1)}, f32[8192]{0:T(1024)}, u32[]{:S(2)}) copy-start(f32[8192]{0:T(1024)} %param.17) | copy-start | bytes 98308
  116.7 53.6 %copy-start.1 = (bf16[8192,64]{0,1:T(8,128)(2,1)S(1)}, bf16[8192,64]{0,1:T(8,128)(2,1)}, u32[]{:S(2)}) copy-start(bf16[8192,64]{0,1:T(8,128)(2,1)} %param.19) | copy-start | bytes 3145732
  176.4 10.8 %all-to-all-start.2 = ((bf16[16,4,640]{2,1,0:T(4,128)(2,1)}), bf16[16,4,640]{2,1,0:T(4,128)(2,1)S(1)}, u32[]{:S(2)}, u32[]{:S(2)}) async-start(bf16[16,4,640]{2,1,0:T(4,128)(2,1)} %pad_maximum_fusion.1), calls=%async_computation.2 | async-start | bytes 163840 | tf_op jit(solution)/shard_map/all_to_all | solution.py:93
  180.0 51.2 %all-gather.15.cloned.1.call-start = ((), (), s32[]{:S(2)}) async-start(), calls=%async_computation.7 | async-start | bytes 1114112 | tf_op jit(solution)/shard_map/all_gather | solution.py:107
  238.2 10.5 %all-to-all-start.3 = ((bf16[16,4,512]{2,1,0:T(4,128)(2,1)}), bf16[16,4,512]{2,1,0:T(4,128)(2,1)S(1)}, u32[]{:S(2)}, u32[]{:S(2)}) async-start(bf16[16,4,512]{2,1,0:T(4,128)(2,1)} %all_to_all.46), calls=%async_computation.3 | async-start | bytes 131072 | tf_op jit(solution)/shard_map/all_to_all | solution.py:112
Sparse Core Ops, SparseCore 0:
  10.7 40.6 all-gather.8
  80.0 35.3 all-gather.10
  133.2 35.2 all-gather.12
  195.9 35.3 all-gather.14
where the time goes:
time: 257 us; the launch traced here: 256 us
  waiting for transfers between devices  167 us (65%)
  matrix products  36.5 us (14%)
  between operations  14.1 us (5%)
  starting transfers between devices  11 us (4%)
  blocking collectives  10.3 us (4%)
  local copies, waits for them, and re-layouts  8.64 us (3%)
  other arithmetic  8.12 us (3%)
    all_gather x2, waiting for transfers between devices, local(): project_segment = lax.all_gather(normed, 'wide', axis=0, tiled=True)  76 us
    all_gather x2, waiting for transfers between devices, local(): lax.all_gather(context, 'wide', axis=0, tiled=True)  70.7 us
    all_to_all x2, waiting for transfers between devices, local(): lax.all_to_all(projected, 'wide', split_axis=0, concat_axis=1, tiled=True)  14.1 us
    all_to_all x1, blocking collectives, local(): lax.all_to_all(attended, 'wide', split_axis=0, concat_axis=1, tiled=True)  10.3 us
    dot_general x2, matrix products, local(): jnp.dot(lax.all_gather(context, 'wide', axis=0, tiled=True), output_weigh...  9.96 us
    dot_general x2, matrix products, local(): jnp.dot(project_segment, query_weight, preferred_element_type=jnp.float32)  9.88 us
    unnamed x17, local copies, waits for them, and re-layouts  7.36 us
    all_to_all x2, starting transfers between devices, local(): lax.all_to_all(projected, 'wide', split_axis=0, concat_axis=1, tiled=True)  7.25 us
  transfers between devices with their start and end apart: 7, of which 7 were waited for; matrix products, arithmetic and copies ran while one was open for 1% of the time, Pallas kernels for 0%

commit v1 on v0

--- a/solution.py
+++ b/solution.py
@@ -1,8 +1,11 @@
 import math
+from functools import partial
 
 import jax
 import jax.numpy as jnp
 from jax import lax
+from jax.experimental import pallas as pl
+from jax.experimental.pallas import tpu as pltpu
 from jax.sharding import PartitionSpec as P
 
 QH = 64
@@ -123,9 +126,411 @@
     return (final_state, new_entries)
 
 
+CHUNKS = 2
+
+
+def copy_to(src, dst, send_sem, recv_sem, peer):
+    return pltpu.make_async_remote_copy(
+        src_ref=src,
+        dst_ref=dst,
+        send_sem=send_sem,
+        recv_sem=recv_sem,
+        device_id={"wide": peer},
+        device_id_type=pl.DeviceIdType.MESH,
+    )
+
+
+def exchange_start(n, me, src, dst, send, recv):
+    def go(o, _):
+        peer = lax.rem(me + o, n)
+        copy_to(src.at[peer], dst.at[me], send.at[o], recv.at[o], peer).start()
+        return 0
+
+    lax.fori_loop(1, n, go, 0)
+    dst[me] = src[me]
+
+
+def exchange_finish(n, me, src, dst, send, recv):
+    def go(o, _):
+        peer = lax.rem(me + o, n)
+        copy = copy_to(src.at[peer], dst.at[lax.rem(me + n - o, n)], send.at[o], recv.at[o], peer)
+        copy.wait_recv()
+        copy.wait_send()
+        return 0
+
+    lax.fori_loop(1, n, go, 0)
+
+
+def ring_index(n, position, core):
+    depth = n // 4
+    y = position // depth
+    z = position + y * (2 * depth - 1 - 2 * position)
+    return (z * 2 + y) * 2 + core
+
+
+def ring_gather(n, me, buf, sems):
+    send, recv, pair_send, pair_recv = sems
+    chips = n // 2
+    depth = n // 4
+    half = chips // 2
+    core = lax.rem(me, 2)
+    chip = me // 2
+    y = lax.rem(chip, 2)
+    z = chip // 2
+    place = z + y * (2 * depth - 1 - 2 * z)
+    sibling = me + 1 - 2 * core
+    rows = buf.shape[1] // CHUNKS
+
+    def at(position):
+        return ring_index(n, lax.rem(position + 2 * chips, chips), core)
+
+    def piece(slot, c):
+        return buf.at[slot, pl.ds(c * rows, rows)]
+
+    def hop(way, h, c):
+        step = 1 if way == 0 else -1
+        slot = at(place - step * h)
+        return copy_to(
+            piece(slot, c), piece(slot, c), send.at[way, h, c], recv.at[way, h, c], at(place + step)
+        )
+
+    def valid(way, h, c):
+        return h < half - 1 or (h == half - 1 and c % 2 == way)
+
+    def pair(way, h, c):
+        step = 1 if way == 0 else -1
+        slot = at(place - step * h)
+        return copy_to(
+            piece(slot, c), piece(slot, c), pair_send.at[way, h, c], pair_recv.at[way, h, c], sibling
+        )
+
+    started, pairs = [], []
+    for c in range(CHUNKS):
+        for way in (0, 1):
+            copy = hop(way, 0, c)
+            copy.start()
+            started.append(copy)
+    for c in range(CHUNKS):
+        copy = pair(0, 0, c)
+        copy.start()
+        pairs.append(copy)
+    for h in range(half):
+        for c in range(CHUNKS):
+            for way in (0, 1):
+                if not valid(way, h, c):
+                    continue
+                hop(way, h, c).wait_recv()
+                if valid(way, h + 1, c):
+                    copy = hop(way, h + 1, c)
+                    copy.start()
+                    started.append(copy)
+                copy = pair(way, h + 1, c)
+                copy.start()
+                pairs.append(copy)
+    for copy in pairs:
+        copy.wait_recv()
+    for copy in started + pairs:
+        copy.wait_send()
+
+
+def layer_kernel(
+    n,
+    x0_ref, gain_ref, freq_ref, lengths_ref, wq_hbm, wk_hbm, wv_hbm, wo_hbm, cache_hbm,
+    out_ref, keys_ref, values_ref,
+    w_ref, wk_ref, wv_ref, wo_ref, cache_ref, xr_ref, xc_ref, xg_ref, pr_ref, m32_ref, sbuf_ref,
+    rbuf_ref, cos_ref, sin_ref, rq_ref, cg_ref, t32_ref, acc_ref, fbuf_ref, fr_ref,
+    load_sem, x_send, x_recv, q_send, q_recv, f_send, f_recv,
+    g_send, g_recv, gp_send, gp_recv, c_send, c_recv, cp_send, cp_recv,
+):
+    me = lax.axis_index("wide")
+    robots = lengths_ref.shape[0]
+    rows = n * robots
+    width = w_ref.shape[0]
+    loads = [
+        pltpu.make_async_copy(wk_hbm, wk_ref, load_sem.at[0]),
+        pltpu.make_async_copy(wv_hbm, wv_ref, load_sem.at[1]),
+        pltpu.make_async_copy(wq_hbm, w_ref.at[:, pl.ds(0, 512)], load_sem.at[2]),
+        pltpu.make_async_copy(cache_hbm, cache_ref, load_sem.at[3]),
+        pltpu.make_async_copy(wo_hbm, wo_ref, load_sem.at[4]),
+    ]
+    for load in loads:
+        load.start()
+    barrier = pltpu.get_barrier_semaphore()
+
+    def greet(o, _):
+        pl.semaphore_signal(
+            barrier, inc=1, device_id={"wide": lax.rem(me + o, n)}, device_id_type=pl.DeviceIdType.MESH
+        )
+        return 0
+
+    lax.fori_loop(1, n, greet, 0)
+    pl.semaphore_wait(barrier, n - 1)
+    exchange_start(n, me, x0_ref, xr_ref, x_send, x_recv)
+
+    robot_of = lax.broadcasted_iota(jnp.int32, (32, 128), 0) % robots
+    lane = lax.broadcasted_iota(jnp.int32, (32, 128), 1)
+    length = jnp.zeros((32, 128), jnp.int32)
+    for r in range(robots):
+        length = jnp.where(robot_of == r, lengths_ref[r], length)
+    for t in range(STEPS):
+        angles = (length + t).astype(jnp.float32) * freq_ref[...]
+        cos_ref[t] = jnp.cos(angles)
+        sine = jnp.sin(angles)
+        sin_ref[t] = jnp.where(lane < HD // 2, -sine, sine)
+    m32_ref[...] = jnp.zeros_like(m32_ref)
+    keys_ref[...] = jnp.zeros_like(keys_ref)
+    values_ref[...] = jnp.zeros_like(values_ref)
+
+    loads[0].wait()
+    loads[1].wait()
+
+    def join(i, _):
+        part = pl.ds(pl.multiple_of(i * 512, 512), 512)
+        w_ref[part, 512:640] = jnp.concatenate([wk_ref[part, :], wv_ref[part, :]], axis=1)
+        return 0
+
+    lax.fori_loop(0, width // 512, join, 0)
+    exchange_finish(n, me, x0_ref, xr_ref, x_send, x_recv)
+    t32_ref[0:256] = xr_ref[...].reshape(256, 128).astype(jnp.float32)
+    for j in range(4):
+        for r in range(robots):
+            xc_ref[pl.ds(rows * j + r, n, stride=robots), :] = t32_ref[
+                pl.ds(4 * j + r, n, stride=16), :
+            ]
+    loads[2].wait()
+
+    def step(t, _):
+        xg_ref[me] = xc_ref[...].astype(jnp.bfloat16)
+        ring_gather(n, me, xg_ref, (g_send, g_recv, gp_send, gp_recv))
+
+        def square(s, total):
+            x = xg_ref[s].astype(jnp.float32)
+            x = x * x
+            for j in range(4):
+                total = total + x[rows * j : rows * j + rows]
+            return total
+
+        total = lax.fori_loop(0, n, square, jnp.zeros((rows, 128), jnp.float32))
+        inverse = lax.rsqrt(jnp.sum(total, axis=1, keepdims=True) / width + norm_eps)
+        inverse = jnp.broadcast_to(inverse, (rows, 128))
+        acc_ref[...] = jnp.zeros_like(acc_ref)
+
+        def project(s, _):
+            parts = []
+            for j in range(4):
+                x = xg_ref[s, rows * j : rows * j + rows].astype(jnp.float32)
+                parts.append((x * inverse * gain_ref[pl.ds(4 * s + j, 1), :]).astype(jnp.bfloat16))
+            acc_ref[...] += jnp.dot(
+                jnp.concatenate(parts, axis=1),
+                w_ref[pl.ds(pl.multiple_of(s * 512, 512), 512), :],
+                preferred_element_type=jnp.float32,
+            )
+            return 0
+
+        lax.fori_loop(0, n, project, 0)
+        for j in range(5):
+            pr_ref[rows * j : rows * j + rows] = acc_ref[:, 128 * j : 128 * j + 128]
+        for j in range(5):
+            for r in range(robots):
+                m32_ref[pl.ds(4 * j + r, n, stride=32), :] = pr_ref[
+                    pl.ds(rows * j + r, n, stride=robots), :
+                ]
+        sbuf_ref[...] = m32_ref[...].reshape(n, 32, 128).astype(jnp.bfloat16)
+        exchange_start(n, me, sbuf_ref, rbuf_ref, q_send, q_recv)
+
+        @pl.when(t == 0)
+        def _():
+            loads[3].wait()
+
+        exchange_finish(n, me, sbuf_ref, rbuf_ref, q_send, q_recv)
+        cosine = cos_ref[t]
+        sine = sin_ref[t]
+        slot = lax.broadcasted_iota(jnp.int32, (8, 512), 1)
+        low = lax.broadcasted_iota(jnp.int32, (8, 128), 1) < HD // 2
+        scale = 1.0 / math.sqrt(HD)
+
+        def attend(g, _):
+            first = rbuf_ref[2 * g].astype(jnp.float32)
+            second = rbuf_ref[2 * g + 1].astype(jnp.float32)
+            q = jnp.concatenate([first[:16], second[:16]], axis=0)
+            q = q * cosine + pltpu.roll(q, HD // 2, 1) * sine
+            rq_ref[...] = q.astype(jnp.bfloat16).astype(jnp.float32)
+            a, b = first[16:24], second[16:24]
+            k = jnp.where(low, a, pltpu.roll(b, HD // 2, 1))
+            v = jnp.where(low, pltpu.roll(a, HD // 2, 1), b)
+            k = k * cosine[:8] + pltpu.roll(k, HD // 2, 1) * sine[:8]
+            keys_ref[t, g] = k.astype(jnp.bfloat16).astype(jnp.float32)
+            values_ref[t, g] = v
+            past, fresh = [], []
+            for r in range(robots):
+                q = rq_ref[pl.ds(r, 8, stride=robots), :]
+                s = lax.dot_general(
+                    q.astype(jnp.bfloat16),
+                    cache_ref[r, 0, g],
+                    (((1,), (1,)), ((), ())),
+                    preferred_element_type=jnp.float32,
+                )
+                past.append(jnp.where(slot < lengths_ref[r], s * scale, -jnp.inf))
+                fresh.append(
+                    [
+                        jnp.sum(q * keys_ref[i, g, r : r + 1, :], axis=1, keepdims=True) * scale
+                        for i in range(STEPS)
+                    ]
+                )
+            past = jnp.concatenate(past, axis=0)
+            fresh = [jnp.concatenate([f[i] for f in fresh], axis=0) for i in range(STEPS)]
+            for i in range(1, STEPS):
+                fresh[i] = jnp.where(i <= t, fresh[i], -jnp.inf)
+            peak = jnp.max(past, axis=1, keepdims=True)
+            for f in fresh:
+                peak = jnp.maximum(peak, f)
+            past = jnp.exp(past - peak)
+            fresh = [jnp.exp(f - peak) for f in fresh]
+            denominator = jnp.sum(past, axis=1, keepdims=True)
+            for f in fresh:
+                denominator = denominator + f
+            past = past / denominator
+            fresh = [(f / denominator).astype(jnp.bfloat16).astype(jnp.float32) for f in fresh]
+            context = []
+            for r in range(robots):
+                c = jnp.dot(
+                    past[8 * r : 8 * r + 8].astype(jnp.bfloat16),
+                    cache_ref[r, 1, g],
+                    preferred_element_type=jnp.float32,
+                )
+                for i in range(STEPS):
+                    c = c + fresh[i][8 * r : 8 * r + 8] * values_ref[i, g, r : r + 1, :]
+                context.append(c)
+            cg_ref[me, pl.ds(pl.multiple_of(g * 32, 32), 32), :] = jnp.concatenate(
+                context, axis=0
+            ).astype(jnp.bfloat16)
+            return 0
+
+        lax.fori_loop(0, KVH, attend, 0)
+
+        @pl.when(t == 0)
+        def _():
+            loads[4].wait()
+
+        ring_gather(n, me, cg_ref, (c_send, c_recv, cp_send, cp_recv))
+        acc_ref[...] = jnp.zeros_like(acc_ref)
+
+        def output(g, _):
+            block = cg_ref[:, pl.ds(pl.multiple_of(g * 32, 32), 32), :]
+            t32_ref[...] = block.reshape(n * 32, 128).astype(jnp.float32)
+            left = jnp.concatenate(
+                [t32_ref[pl.ds(h, rows, stride=8), :].astype(jnp.bfloat16) for h in range(8)], axis=1
+            )
+            acc_ref[:, 0:512] += jnp.dot(
+                left,
+                wo_ref[pl.ds(pl.multiple_of(g * 1024, 1024), 1024), :],
+                preferred_element_type=jnp.float32,
+            )
+            return 0
+
+        lax.fori_loop(0, KVH, output, 0)
+        for j in range(4):
+            part = slice(rows * j, rows * j + rows)
+            attended = acc_ref[:, 128 * j : 128 * j + 128].astype(jnp.bfloat16).astype(jnp.float32)
+            xc_ref[part] = (xc_ref[part] + attended).astype(jnp.bfloat16).astype(jnp.float32)
+        return 0
+
+    lax.fori_loop(0, STEPS, step, 0)
+    for j in range(4):
+        for r in range(robots):
+            t32_ref[pl.ds(4 * j + r, n, stride=16), :] = xc_ref[
+                pl.ds(rows * j + r, n, stride=robots), :
+            ]
+    fbuf_ref[...] = t32_ref[0:256].reshape(n, 16, 128).astype(jnp.bfloat16)
+    exchange_start(n, me, fbuf_ref, fr_ref, f_send, f_recv)
+    exchange_finish(n, me, fbuf_ref, fr_ref, f_send, f_recv)
+    t32_ref[0:256] = fr_ref[...].reshape(256, 128).astype(jnp.float32)
+    for r in range(robots):
+        out_ref[64 * r : 64 * r + 64] = t32_ref[pl.ds(r, 64, stride=robots), :].astype(jnp.bfloat16)
+
+
+def fused(
+    residual, norm_gain, query_weight, key_weight, value_weight, output_weight, past_cache, lengths
+):
+    n = lax.axis_size("wide")
+    robots, width = residual.shape
+    frequency = rope_base ** (-2.0 * jnp.arange(HD // 2, dtype=jnp.float32) / HD)
+    frequency = jnp.concatenate([frequency, frequency])[None, :]
+    x0 = residual.reshape(robots, n, 4, 128).transpose(1, 2, 0, 3).reshape(n, 16, 128)
+    vmem = pl.BlockSpec(memory_space=pltpu.VMEM)
+    smem = pl.BlockSpec(memory_space=pltpu.SMEM)
+    any_spec = pl.BlockSpec(memory_space=pl.ANY)
+    bf16, f32 = jnp.bfloat16, jnp.float32
+    dma = pltpu.SemaphoreType.DMA
+    half = n // 4
+    ring_sems = [
+        dma((2, half, CHUNKS)),
+        dma((2, half, CHUNKS)),
+        dma((2, half + 1, CHUNKS)),
+        dma((2, half + 1, CHUNKS)),
+    ]
+    out, keys, values = pl.pallas_call(
+        partial(layer_kernel, n),
+        out_shape=(
+            jax.ShapeDtypeStruct((robots * 64, 128), bf16),
+            jax.ShapeDtypeStruct((STEPS, KVH, 8, HD), f32),
+            jax.ShapeDtypeStruct((STEPS, KVH, 8, HD), f32),
+        ),
+        in_specs=[vmem, vmem, vmem, smem] + [any_spec] * 5,
+        out_specs=(vmem, vmem, vmem),
+        scratch_shapes=[
+            pltpu.VMEM((width, 640), bf16),
+            pltpu.VMEM(key_weight.shape, bf16),
+            pltpu.VMEM(value_weight.shape, bf16),
+            pltpu.VMEM(output_weight.shape, bf16),
+            pltpu.VMEM(past_cache.shape, bf16),
+            pltpu.VMEM((n, 16, 128), bf16),
+            pltpu.VMEM((n * 16, 128), f32),
+            pltpu.VMEM((n, n * 16, 128), bf16),
+            pltpu.VMEM((5 * n * robots, 128), f32),
+            pltpu.VMEM((n * 32, 128), f32),
+            pltpu.VMEM((n, 32, 128), bf16),
+            pltpu.VMEM((n, 32, 128), bf16),
+            pltpu.VMEM((STEPS, 32, 128), f32),
+            pltpu.VMEM((STEPS, 32, 128), f32),
+            pltpu.VMEM((32, 128), f32),
+            pltpu.VMEM((n, KVH * 32, 128), bf16),
+            pltpu.VMEM((n * 32, 128), f32),
+            pltpu.VMEM((n * robots, 640), f32),
+            pltpu.VMEM((n, 16, 128), bf16),
+            pltpu.VMEM((n, 16, 128), bf16),
+            dma((5,)),
+            dma((n,)), dma((n,)), dma((n,)), dma((n,)), dma((n,)), dma((n,)),
+        ]
+        + ring_sems
+        + ring_sems,
+        compiler_params=pltpu.CompilerParams(
+            collective_id=0, has_side_effects=True, vmem_limit_bytes=58 * 1024 * 1024
+        ),
+    )(
+        x0, norm_gain.reshape(width // 128, 128), frequency, lengths,
+        query_weight, key_weight, value_weight, output_weight, past_cache,
+    )
+    entries = jnp.stack([keys[:, :, :robots], values[:, :, :robots]], axis=1)
+    entries = entries.transpose(3, 0, 1, 2, 4).reshape(robots, STEPS, 2 * KVH * HD)
+    return out.reshape(robots, width), entries.astype(bf16)
+
+
+def dispatch(*arrays):
+    residual, _, query_weight, key_weight, _, _, past_cache, _ = arrays
+    fits = (
+        lax.axis_size("wide") == 16
+        and residual.shape == (4, 8192)
+        and query_weight.shape[1] == 512
+        and key_weight.shape[1] == 64
+        and past_cache.shape[1:] == (2, KVH, 512, HD)
+    )
+    return fused(*arrays) if fits else local(*arrays)
+
+
 def solution(mesh):
     return jax.shard_map(
-        local,
+        dispatch,
         mesh=mesh,
         in_specs=(
             P(("groups", "wide"), None),

time: 257 us -> 119 us (0.46)
  waiting for transfers between devices: 167 us -> 0 us
  Pallas kernels: 0 us -> 109 us
  matrix products: 36.5 us -> 0 us
  between operations: 14.1 us -> 0.66 us
  starting transfers between devices: 11 us -> 0 us
  blocking collectives: 10.3 us -> 0 us
  other arithmetic: 8.12 us -> 0.63 us
    all_gather x4 -> x0, waiting for transfers between devices: 147 us -> none  [the longest x2 76 us: local(): project_segment = lax.all_gather(normed, 'wide', axis=0, tiled=True)]
    pallas_call x0 -> x1, Pallas kernels: none -> 109 us  [fused(): pl.pallas_call(partial(layer_kernel, n), out_shape=(jax.ShapeDtypeStruct(...]
    dot_general x16 -> x0, matrix products: 36.5 us -> none  [the longest x2 9.96 us: local(): jnp.dot(lax.all_gather(context, 'wide', axis=0, tiled=True), output_weigh...]
    all_to_all x3 -> x0, waiting for transfers between devices: 20.3 us -> none  [the longest x2 14.1 us: local(): lax.all_to_all(projected, 'wide', split_axis=0, concat_axis=1, tiled=True)]
    all_to_all x3 -> x0, starting transfers between devices: 10.9 us -> none  [the longest x2 7.25 us: local(): lax.all_to_all(projected, 'wide', split_axis=0, concat_axis=1, tiled=True)]
    all_to_all x1 -> x0, blocking collectives: 10.3 us -> none  [local(): lax.all_to_all(attended, 'wide', split_axis=0, concat_axis=1, tiled=True)]
    unnamed x17 -> x2, local copies, waits for them, and re-layouts: 7.36 us -> 5.49 us
  transfers between devices with their start and end apart: 7 -> 0, of which waited for: 7 -> 0; matrix products, arithmetic and copies ran while one was open for 1% -> 0% of each run, Pallas kernels for 0% -> 0%
where the time goes in v1:
time: 119 us
  Pallas kernels  109 us (92%)
  local copies, waits for them, and re-layouts  8.5 us (7%)
    pallas_call x1, Pallas kernels, fused(): pl.pallas_call(partial(layer_kernel, n), out_shape=(jax.ShapeDtypeStruct(...  109 us
    unnamed x2, local copies, waits for them, and re-layouts  5.49 us

profile of v1, /device:TPU:0, one launch (start us, length us, event | category | flops | bytes accessed | tf_op | source)
XLA Modules:
  0.0 118.9 jit_solution(14037980803806721944)
XLA Ops:
  0.6 0.6 maximum_bitcast_fusion.1.freq_ref
  1.2 2.8 %copy.14.wk_hbm = bf16[8192,64]{1,0:T(8,128)(2,1)} copy(bf16[8192,64]{0,1:T(8,128)(2,1)} %param.11) | data formatting | bytes 2097152 | tf_op args[3]
  4.0 2.7 %copy.15.wv_hbm = bf16[8192,64]{1,0:T(8,128)(2,1)} copy(bf16[8192,64]{0,1:T(8,128)(2,1)} %param.12) | data formatting | bytes 2097152 | tf_op args[4]
  6.7 109.1 %shard_map.95 = (bf16[256,128]{1,0:T(8,128)(2,1)}, f32[2,8,8,128]{3,2,1,0:T(8,128)}, f32[2,8,8,128]{3,2,1,0:T(8,128)}) custom-call(bf16[16,16,128]{2,1,0:T(8,128)(2,1)} %bitcast.16, f32[64,128]{1,0:T(8,128)} %bitcast.17, f32[1,128]{1,0:T(1,128)} %maximum_bitcast_fusion.1.freq_ref, s32[4]{0:T(128)} %lengths_ref.1, bf16[8192,512]{1,0:T(8,128)(2,1)} %wq_hbm.1, ...), custom_call_target="tpu_custom_call" | custom-call | tf_op jit(solution)/shard_map/pallas_call | solution.py:472
  115.9 1.5 %reshape.21 = bf16[4,8192]{1,0:T(4,128)(2,1)} reshape(bf16[256,128]{1,0:T(8,128)(2,1)} %get-tuple-element.5) | data formatting | bytes 131072 | tf_op jit(solution)/shard_map/reshape | solution.py:516
  117.4 0.9 fusion
  118.3 0.6 convert_element_type.8
  (3 shorter events, 0.0 us)

commit v2 on v1

--- a/solution.py
+++ b/solution.py
@@ -3,6 +3,7 @@
 
 import jax
 import jax.numpy as jnp
+import numpy as np
 from jax import lax
 from jax.experimental import pallas as pl
 from jax.experimental.pallas import tpu as pltpu
@@ -126,9 +127,6 @@
     return (final_state, new_entries)
 
 
-CHUNKS = 2
-
-
 def copy_to(src, dst, send_sem, recv_sem, peer):
     return pltpu.make_async_remote_copy(
         src_ref=src,
@@ -161,95 +159,69 @@
     lax.fori_loop(1, n, go, 0)
 
 
-def ring_index(n, position, core):
-    depth = n // 4
-    y = position // depth
-    z = position + y * (2 * depth - 1 - 2 * position)
-    return (z * 2 + y) * 2 + core
-
-
-def ring_gather(n, me, buf, sems):
-    send, recv, pair_send, pair_recv = sems
-    chips = n // 2
-    depth = n // 4
-    half = chips // 2
-    core = lax.rem(me, 2)
-    chip = me // 2
-    y = lax.rem(chip, 2)
-    z = chip // 2
-    place = z + y * (2 * depth - 1 - 2 * z)
-    sibling = me + 1 - 2 * core
-    rows = buf.shape[1] // CHUNKS
-
-    def at(position):
-        return ring_index(n, lax.rem(position + 2 * chips, chips), core)
-
-    def piece(slot, c):
-        return buf.at[slot, pl.ds(c * rows, rows)]
-
-    def hop(way, h, c):
-        step = 1 if way == 0 else -1
-        slot = at(place - step * h)
-        return copy_to(
-            piece(slot, c), piece(slot, c), send.at[way, h, c], recv.at[way, h, c], at(place + step)
-        )
-
-    def valid(way, h, c):
-        return h < half - 1 or (h == half - 1 and c % 2 == way)
-
-    def pair(way, h, c):
-        step = 1 if way == 0 else -1
-        slot = at(place - step * h)
-        return copy_to(
-            piece(slot, c), piece(slot, c), pair_send.at[way, h, c], pair_recv.at[way, h, c], sibling
-        )
-
-    started, pairs = [], []
-    for c in range(CHUNKS):
-        for way in (0, 1):
-            copy = hop(way, 0, c)
-            copy.start()
-            started.append(copy)
-    for c in range(CHUNKS):
-        copy = pair(0, 0, c)
-        copy.start()
-        pairs.append(copy)
-    for h in range(half):
-        for c in range(CHUNKS):
-            for way in (0, 1):
-                if not valid(way, h, c):
-                    continue
-                hop(way, h, c).wait_recv()
-                if valid(way, h + 1, c):
-                    copy = hop(way, h + 1, c)
-                    copy.start()
-                    started.append(copy)
-                copy = pair(way, h + 1, c)
-                copy.start()
-                pairs.append(copy)
-    for copy in pairs:
-        copy.wait_recv()
-    for copy in started + pairs:
-        copy.wait_send()
+PIECES = 4
+LAG = 2
+
+
+class Gather:
+    def __init__(self, n, me, buf, sems, pieces):
+        self.n, self.me, self.buf = n, me, buf
+        self.send, self.recv, self.pair_send, self.pair_recv = sems
+        self.chips = n // 2
+        self.rows = buf.shape[1] // pieces
+        self.order = sorted(range(1, self.chips), key=lambda o: min(o, self.chips - o))
+
+    def part(self, slot, c):
+        return self.buf.at[slot, pl.ds(pl.multiple_of(c * self.rows, self.rows), self.rows)]
+
+    def far(self, o, c):
+        part = self.part(self.me, c)
+        peer = lax.rem(self.me + 2 * o, self.n)
+        return copy_to(part, part, self.send.at[c, o], self.recv.at[c, o], peer)
+
+    def near(self, o, c):
+        part = self.part(lax.rem(self.me + self.n - 2 * o, self.n), c)
+        sibling = self.me + 1 - 2 * lax.rem(self.me, 2)
+        return copy_to(part, part, self.pair_send.at[c, o], self.pair_recv.at[c, o], sibling)
+
+    def start(self, c):
+        for o in self.order[::-1]:
+            self.far(o, c).start()
+        self.near(0, c).start()
+
+    def forward(self, c):
+        for o in self.order:
+            self.far(o, c).wait_recv()
+            self.near(o, c).start()
+
+    def arrive(self, c):
+        for o in range(self.chips):
+            self.near(o, c).wait_recv()
+
+    def drain(self, c):
+        self.near(0, c).wait_send()
+        for o in self.order:
+            self.far(o, c).wait_send()
+            self.near(o, c).wait_send()
 
 
 def layer_kernel(
     n,
     x0_ref, gain_ref, freq_ref, lengths_ref, wq_hbm, wk_hbm, wv_hbm, wo_hbm, cache_hbm,
     out_ref, keys_ref, values_ref,
-    w_ref, wk_ref, wv_ref, wo_ref, cache_ref, xr_ref, xc_ref, xg_ref, pr_ref, m32_ref, sbuf_ref,
+    wq_ref, wkv_ref, wo_ref, cache_ref, xr_ref, xc_ref, xg_ref, pr_ref, m32_ref, sbuf_ref,
     rbuf_ref, cos_ref, sin_ref, rq_ref, cg_ref, t32_ref, acc_ref, fbuf_ref, fr_ref,
     load_sem, x_send, x_recv, q_send, q_recv, f_send, f_recv,
-    g_send, g_recv, gp_send, gp_recv, c_send, c_recv, cp_send, cp_recv,
+    *gather_sems,
 ):
     me = lax.axis_index("wide")
     robots = lengths_ref.shape[0]
     rows = n * robots
-    width = w_ref.shape[0]
+    width = wq_ref.shape[0]
     loads = [
-        pltpu.make_async_copy(wk_hbm, wk_ref, load_sem.at[0]),
-        pltpu.make_async_copy(wv_hbm, wv_ref, load_sem.at[1]),
-        pltpu.make_async_copy(wq_hbm, w_ref.at[:, pl.ds(0, 512)], load_sem.at[2]),
+        pltpu.make_async_copy(wk_hbm, wkv_ref.at[pl.ds(0, 64)], load_sem.at[0]),
+        pltpu.make_async_copy(wv_hbm, wkv_ref.at[pl.ds(64, 64)], load_sem.at[1]),
+        pltpu.make_async_copy(wq_hbm, wq_ref, load_sem.at[2]),
         pltpu.make_async_copy(cache_hbm, cache_ref, load_sem.at[3]),
         pltpu.make_async_copy(wo_hbm, wo_ref, load_sem.at[4]),
     ]
@@ -264,8 +236,11 @@
         return 0
 
     lax.fori_loop(1, n, greet, 0)
+    for k in range(4 * n):
+        t32_ref[4 * k : 4 * k + 4] = x0_ref[:, 128 * k : 128 * k + 128].astype(jnp.float32)
+    fbuf_ref[...] = t32_ref[0:256].reshape(n, 16, 128).astype(jnp.bfloat16)
     pl.semaphore_wait(barrier, n - 1)
-    exchange_start(n, me, x0_ref, xr_ref, x_send, x_recv)
+    exchange_start(n, me, fbuf_ref, xr_ref, x_send, x_recv)
 
     robot_of = lax.broadcasted_iota(jnp.int32, (32, 128), 0) % robots
     lane = lax.broadcasted_iota(jnp.int32, (32, 128), 1)
@@ -281,27 +256,24 @@
     keys_ref[...] = jnp.zeros_like(keys_ref)
     values_ref[...] = jnp.zeros_like(values_ref)
 
-    loads[0].wait()
-    loads[1].wait()
-
-    def join(i, _):
-        part = pl.ds(pl.multiple_of(i * 512, 512), 512)
-        w_ref[part, 512:640] = jnp.concatenate([wk_ref[part, :], wv_ref[part, :]], axis=1)
-        return 0
-
-    lax.fori_loop(0, width // 512, join, 0)
-    exchange_finish(n, me, x0_ref, xr_ref, x_send, x_recv)
+    exchange_finish(n, me, fbuf_ref, xr_ref, x_send, x_recv)
     t32_ref[0:256] = xr_ref[...].reshape(256, 128).astype(jnp.float32)
     for j in range(4):
         for r in range(robots):
             xc_ref[pl.ds(rows * j + r, n, stride=robots), :] = t32_ref[
                 pl.ds(4 * j + r, n, stride=16), :
             ]
-    loads[2].wait()
+    for load in loads[:3]:
+        load.wait()
+
+    columns = Gather(n, me, xg_ref, gather_sems[:4], 1)
+    contexts = Gather(n, me, cg_ref, gather_sems[4:], PIECES)
 
     def step(t, _):
         xg_ref[me] = xc_ref[...].astype(jnp.bfloat16)
-        ring_gather(n, me, xg_ref, (g_send, g_recv, gp_send, gp_recv))
+        columns.start(0)
+        columns.forward(0)
+        columns.arrive(0)
 
         def square(s, total):
             x = xg_ref[s].astype(jnp.float32)
@@ -320,9 +292,15 @@
             for j in range(4):
                 x = xg_ref[s, rows * j : rows * j + rows].astype(jnp.float32)
                 parts.append((x * inverse * gain_ref[pl.ds(4 * s + j, 1), :]).astype(jnp.bfloat16))
-            acc_ref[...] += jnp.dot(
-                jnp.concatenate(parts, axis=1),
-                w_ref[pl.ds(pl.multiple_of(s * 512, 512), 512), :],
+            normed = jnp.concatenate(parts, axis=1)
+            part = pl.ds(pl.multiple_of(s * 512, 512), 512)
+            acc_ref[:, 0:512] += jnp.dot(
+                normed, wq_ref[part, :], preferred_element_type=jnp.float32
+            )
+            acc_ref[:, 512:640] += lax.dot_general(
+                normed,
+                wkv_ref[:, part],
+                (((1,), (1,)), ((), ())),
                 preferred_element_type=jnp.float32,
             )
             return 0
@@ -342,6 +320,7 @@
         def _():
             loads[3].wait()
 
+        columns.drain(0)
         exchange_finish(n, me, sbuf_ref, rbuf_ref, q_send, q_recv)
         cosine = cos_ref[t]
         sine = sin_ref[t]
@@ -406,13 +385,24 @@
             ).astype(jnp.bfloat16)
             return 0
 
-        lax.fori_loop(0, KVH, attend, 0)
+        each = KVH // PIECES
+
+        def attend_piece(c, _):
+            lax.fori_loop(c * each, c * each + each, attend, 0)
+            contexts.start(c)
+
+            @pl.when(c >= LAG)
+            def _():
+                contexts.forward(c - LAG)
+
+            return 0
+
+        lax.fori_loop(0, PIECES, attend_piece, 0)
 
         @pl.when(t == 0)
         def _():
             loads[4].wait()
 
-        ring_gather(n, me, cg_ref, (c_send, c_recv, cp_send, cp_recv))
         acc_ref[...] = jnp.zeros_like(acc_ref)
 
         def output(g, _):
@@ -428,11 +418,26 @@
             )
             return 0
 
-        lax.fori_loop(0, KVH, output, 0)
+        def output_piece(c, _):
+            @pl.when(c + PIECES - LAG < PIECES)
+            def _():
+                contexts.forward(c + PIECES - LAG)
+
+            contexts.arrive(c)
+            lax.fori_loop(c * each, c * each + each, output, 0)
+            return 0
+
+        lax.fori_loop(0, PIECES, output_piece, 0)
         for j in range(4):
             part = slice(rows * j, rows * j + rows)
             attended = acc_ref[:, 128 * j : 128 * j + 128].astype(jnp.bfloat16).astype(jnp.float32)
             xc_ref[part] = (xc_ref[part] + attended).astype(jnp.bfloat16).astype(jnp.float32)
+
+        def drain(c, _):
+            contexts.drain(c)
+            return 0
+
+        lax.fori_loop(0, PIECES, drain, 0)
         return 0
 
     lax.fori_loop(0, STEPS, step, 0)
@@ -445,8 +450,8 @@
     exchange_start(n, me, fbuf_ref, fr_ref, f_send, f_recv)
     exchange_finish(n, me, fbuf_ref, fr_ref, f_send, f_recv)
     t32_ref[0:256] = fr_ref[...].reshape(256, 128).astype(jnp.float32)
-    for r in range(robots):
-        out_ref[64 * r : 64 * r + 64] = t32_ref[pl.ds(r, 64, stride=robots), :].astype(jnp.bfloat16)
+    for k in range(4 * n):
+        out_ref[:, 128 * k : 128 * k + 128] = t32_ref[4 * k : 4 * k + 4].astype(jnp.bfloat16)
 
 
 def fused(
@@ -454,34 +459,26 @@
 ):
     n = lax.axis_size("wide")
     robots, width = residual.shape
-    frequency = rope_base ** (-2.0 * jnp.arange(HD // 2, dtype=jnp.float32) / HD)
-    frequency = jnp.concatenate([frequency, frequency])[None, :]
-    x0 = residual.reshape(robots, n, 4, 128).transpose(1, 2, 0, 3).reshape(n, 16, 128)
+    frequency = np.tile(rope_base ** (-2.0 * np.arange(HD // 2) / HD), 2)
+    frequency = jnp.asarray(frequency[None, :], jnp.float32)
     vmem = pl.BlockSpec(memory_space=pltpu.VMEM)
     smem = pl.BlockSpec(memory_space=pltpu.SMEM)
     any_spec = pl.BlockSpec(memory_space=pl.ANY)
     bf16, f32 = jnp.bfloat16, jnp.float32
     dma = pltpu.SemaphoreType.DMA
-    half = n // 4
-    ring_sems = [
-        dma((2, half, CHUNKS)),
-        dma((2, half, CHUNKS)),
-        dma((2, half + 1, CHUNKS)),
-        dma((2, half + 1, CHUNKS)),
-    ]
+    gather_sems = [dma((1, n // 2))] * 4 + [dma((PIECES, n // 2))] * 4
     out, keys, values = pl.pallas_call(
         partial(layer_kernel, n),
         out_shape=(
-            jax.ShapeDtypeStruct((robots * 64, 128), bf16),
+            jax.ShapeDtypeStruct((robots, width), bf16),
             jax.ShapeDtypeStruct((STEPS, KVH, 8, HD), f32),
             jax.ShapeDtypeStruct((STEPS, KVH, 8, HD), f32),
         ),
         in_specs=[vmem, vmem, vmem, smem] + [any_spec] * 5,
         out_specs=(vmem, vmem, vmem),
         scratch_shapes=[
-            pltpu.VMEM((width, 640), bf16),
-            pltpu.VMEM(key_weight.shape, bf16),
-            pltpu.VMEM(value_weight.shape, bf16),
+            pltpu.VMEM(query_weight.shape, bf16),
+            pltpu.VMEM((2 * key_weight.shape[1], width), bf16),
             pltpu.VMEM(output_weight.shape, bf16),
             pltpu.VMEM(past_cache.shape, bf16),
             pltpu.VMEM((n, 16, 128), bf16),
@@ -502,18 +499,17 @@
             dma((5,)),
             dma((n,)), dma((n,)), dma((n,)), dma((n,)), dma((n,)), dma((n,)),
         ]
-        + ring_sems
-        + ring_sems,
+        + gather_sems,
         compiler_params=pltpu.CompilerParams(
             collective_id=0, has_side_effects=True, vmem_limit_bytes=58 * 1024 * 1024
         ),
     )(
-        x0, norm_gain.reshape(width // 128, 128), frequency, lengths,
-        query_weight, key_weight, value_weight, output_weight, past_cache,
+        residual, norm_gain.reshape(width // 128, 128), frequency, lengths,
+        query_weight, key_weight.T, value_weight.T, output_weight, past_cache,
     )
     entries = jnp.stack([keys[:, :, :robots], values[:, :, :robots]], axis=1)
     entries = entries.transpose(3, 0, 1, 2, 4).reshape(robots, STEPS, 2 * KVH * HD)
-    return out.reshape(robots, width), entries.astype(bf16)
+    return out, entries.astype(bf16)
 
 
 def dispatch(*arrays):

time: 119 us -> 102 us (0.86)
  Pallas kernels: 109 us -> 98 us
  local copies, waits for them, and re-layouts: 8.5 us -> 3.01 us
    pallas_call x1, Pallas kernels: 109 us -> 98 us  [fused(): pl.pallas_call(partial(layer_kernel, n), out_shape=(jax.ShapeDtypeStruct(...]
    unnamed x2 -> x1, local copies, waits for them, and re-layouts: 5.49 us -> 1.49 us
    reshape x1 -> x0, local copies, waits for them, and re-layouts: 1.49 us -> none  [fused(): return (out.reshape(robots, width), entries.astype(bf16))]
where the time goes in v2:
time: 102 us
  Pallas kernels  98 us (96%)
  local copies, waits for them, and re-layouts  3.01 us (3%)
    pallas_call x1, Pallas kernels, fused(): pl.pallas_call(partial(layer_kernel, n), out_shape=(jax.ShapeDtypeStruct(...  98 us

profile of v2, /device:TPU:0, one launch (start us, length us, event | category | flops | bytes accessed | tf_op | source)
XLA Modules:
  0.0 101.7 jit_solution(3256804021463767426)
XLA Ops:
  0.6 98.0 %shard_map.104 = (bf16[4,8192]{1,0:T(4,128)(2,1)}, f32[2,8,8,128]{3,2,1,0:T(8,128)}, f32[2,8,8,128]{3,2,1,0:T(8,128)}) custom-call(bf16[4,8192]{1,0:T(4,128)(2,1)} %x0_ref.1, f32[64,128]{1,0:T(8,128)} %bitcast.13, f32[1,128]{1,0:T(1,128)} %constant.2.clone.freq_ref, s32[4]{0:T(128)} %lengths_ref.1, bf16[8192,512]{1,0:T(8,128)(2,1)} %wq_hbm.1, ...), custom_call_target="tpu_custom_call" | custom-call | tf_op jit(solution)/shard_map/pallas_call | solution.py:470
  98.7 0.9 fusion
  99.6 0.6 convert_element_type.8
  100.2 1.5 %copy.13 = bf16[4,8192]{1,0:T(4,128)(2,1)} copy(bf16[4,8192]{1,0:T(4,128)(2,1)} %get-tuple-element.12) | data formatting | bytes 131072
  (2 shorter events, 0.0 us)

commit v3 on v2

--- a/solution.py
+++ b/solution.py
@@ -144,7 +144,7 @@
         copy_to(src.at[peer], dst.at[me], send.at[o], recv.at[o], peer).start()
         return 0
 
-    lax.fori_loop(1, n, go, 0)
+    lax.fori_loop(1, n, go, 0, unroll=True)
     dst[me] = src[me]
 
 
@@ -156,7 +156,7 @@
         copy.wait_send()
         return 0
 
-    lax.fori_loop(1, n, go, 0)
+    lax.fori_loop(1, n, go, 0, unroll=True)
 
 
 PIECES = 4
@@ -282,7 +282,7 @@
                 total = total + x[rows * j : rows * j + rows]
             return total
 
-        total = lax.fori_loop(0, n, square, jnp.zeros((rows, 128), jnp.float32))
+        total = lax.fori_loop(0, n, square, jnp.zeros((rows, 128), jnp.float32), unroll=4)
         inverse = lax.rsqrt(jnp.sum(total, axis=1, keepdims=True) / width + norm_eps)
         inverse = jnp.broadcast_to(inverse, (rows, 128))
         acc_ref[...] = jnp.zeros_like(acc_ref)
@@ -305,7 +305,7 @@
             )
             return 0
 
-        lax.fori_loop(0, n, project, 0)
+        lax.fori_loop(0, n, project, 0, unroll=4)
         for j in range(5):
             pr_ref[rows * j : rows * j + rows] = acc_ref[:, 128 * j : 128 * j + 128]
         for j in range(5):
@@ -388,7 +388,7 @@
         each = KVH // PIECES
 
         def attend_piece(c, _):
-            lax.fori_loop(c * each, c * each + each, attend, 0)
+            [attend(c * each + i, 0) for i in range(each)]
             contexts.start(c)
 
             @pl.when(c >= LAG)
@@ -424,7 +424,7 @@
                 contexts.forward(c + PIECES - LAG)
 
             contexts.arrive(c)
-            lax.fori_loop(c * each, c * each + each, output, 0)
+            [output(c * each + i, 0) for i in range(each)]
             return 0
 
         lax.fori_loop(0, PIECES, output_piece, 0)

time: 102 us -> 97.9 us (0.960)
  Pallas kernels: 98 us -> 94 us
    pallas_call x1, Pallas kernels: 98 us -> 94 us  [fused(): pl.pallas_call(partial(layer_kernel, n), out_shape=(jax.ShapeDtypeStruct(...]
where the time goes in v3:
time: 97.9 us; the launch traced here: 97.7 us
  Pallas kernels  94 us (96%)
  local copies, waits for them, and re-layouts  3.01 us (3%)
    pallas_call x1, Pallas kernels, fused(): pl.pallas_call(partial(layer_kernel, n), out_shape=(jax.ShapeDtypeStruct(...  94 us

profile of v3, /device:TPU:0, one launch (start us, length us, event | category | flops | bytes accessed | tf_op | source)
XLA Modules:
  0.0 97.7 jit_solution(3757251667082892823)
XLA Ops:
  0.6 94.0 %shard_map.104 = (bf16[4,8192]{1,0:T(4,128)(2,1)}, f32[2,8,8,128]{3,2,1,0:T(8,128)}, f32[2,8,8,128]{3,2,1,0:T(8,128)}) custom-call(bf16[4,8192]{1,0:T(4,128)(2,1)} %x0_ref.1, f32[64,128]{1,0:T(8,128)} %bitcast.13, f32[1,128]{1,0:T(1,128)} %constant.2.clone.freq_ref, s32[4]{0:T(128)} %lengths_ref.1, bf16[8192,512]{1,0:T(8,128)(2,1)} %wq_hbm.1, ...), custom_call_target="tpu_custom_call" | custom-call | tf_op jit(solution)/shard_map/pallas_call | solution.py:470
  94.6 0.9 fusion
  95.6 0.6 convert_element_type.8
  96.2 1.5 %copy.13 = bf16[4,8192]{1,0:T(4,128)(2,1)} copy(bf16[4,8192]{1,0:T(4,128)(2,1)} %get-tuple-element.12) | data formatting | bytes 131072
  (2 shorter events, 0.0 us)
